TPU v7x, 32 devices: a whole 2x2x4 slice. The times are simulated.
32 devices in a mesh: groups: 2 (over y), blk: 4 (over z), fsdp: 4 (over x, core).
Axes of the slice: x: 2, y: 2, z: 4, core: 2. Of those that a mesh axis runs over, the one named last changes fastest.
Arguments:
- hidden: bfloat16 [8192, 4096], P(('groups', 'blk', 'fsdp')), parts along dimension 0, may hold values from -6 to 6
- query: bfloat16 [8192, 4096], P(('groups', 'blk', 'fsdp')), parts along dimension 0, may hold values from -1024 to 1024
- out_grad: bfloat16 [8192, 4096], P(('groups', 'blk', 'fsdp')), parts along dimension 0, may hold values from -6 to 6
- lengths: int32 [128], P(('groups', 'blk', 'fsdp')), parts along dimension 0, may hold values from 16 to 63
- gain: float32 [4096], replicated, may hold values from 0.5 to 1.5
- w_key: bfloat16 [4096, 1024], P('fsdp'), may hold values from -0.09375 to 0.09375
- w_value: bfloat16 [4096, 1024], P('fsdp'), may hold values from -0.09375 to 0.09375
- proj_in: bfloat16 [4096, 32], replicated, may hold values from -0.09375 to 0.09375
- proj_out: bfloat16 [1024, 32], replicated, may hold values from -0.1875 to 0.1875
- test_feats: bfloat16 [512, 1024], P('blk'), may hold values from -0.75 to 0.75
Outputs:
- scores: float32 [128, 512], P(('groups', 'blk', 'fsdp')), parts along dimension 0
There are 2 independent parts, one for each index of `groups`. A program takes and returns all parts, laid end to end along the dimension named above; an argument that names none is the same for every part. Nothing has to cross between parts.
All inputs are finite; a program needn't handle non-finite values.
Results may differ from a plain program's by a relative error of at most 0.011.
Values may be sent and summed in bfloat16 or wider, within the bound.
A program may use at most 128 MiB of HBM per device.

v0:
```python
import math

import jax
import jax.numpy as jnp
from jax import lax
from jax.experimental import pallas as pl
from jax.experimental.pallas import tpu as pltpu
from jax.sharding import PartitionSpec as P

HEADS = 32
KV_HEADS = 8
HEAD = 128
PROJ = 32
SEQ = 64


norm_eps = 1e-05
rope_base = 500000.0
damping = 0.01


def swap_halves(block):
    middle = block.shape[-1] // 2
    return jnp.concatenate([block[..., middle:], block[..., :middle]], axis=-1)


def rope_tables():
    places = jnp.arange(SEQ).astype(jnp.float32)
    freqs = rope_base ** (-2.0 * jnp.arange(HEAD // 2).astype(jnp.float32) / HEAD)
    angles = places[:, None] * freqs[None, :]
    cosine = jnp.cos(angles)
    sine_tab = jnp.sin(angles)
    return (jnp.concatenate([cosine, cosine], -1), jnp.concatenate([-sine_tab, sine_tab], -1))


def normalize(hidden, gain):
    widened = hidden.astype(jnp.float32)
    inverse = lax.rsqrt(jnp.mean(widened * widened, axis=1, keepdims=True) + norm_eps)
    return (widened * inverse * gain).astype(jnp.bfloat16)


def features_of(normed, keys_raw, values_raw, query, out_grad, lengths, proj_in, proj_out):
    count = lengths.shape[0]
    group_size = HEADS // KV_HEADS
    cosine, sine_tab = rope_tables()
    keys_raw = keys_raw.reshape(count, SEQ, KV_HEADS, HEAD)
    keys_rot = (
        keys_raw * cosine[None, :, None, :] + swap_halves(keys_raw) * sine_tab[None, :, None, :]
    ).astype(jnp.bfloat16)
    values = values_raw.reshape(count, SEQ, KV_HEADS, HEAD).astype(jnp.bfloat16)
    queries = query.reshape(count, SEQ, KV_HEADS, group_size, HEAD)
    places = jnp.arange(SEQ)
    inside = places[None, :] < lengths[:, None]
    grad_out = jnp.where(
        inside[:, :, None, None, None],
        out_grad.reshape(count, SEQ, KV_HEADS, group_size, HEAD),
        jnp.zeros((), jnp.bfloat16),
    )
    inverse = 1.0 / math.sqrt(HEAD)
    logits = (
        jnp.einsum("eskgh,etkh->ekgst", queries, keys_rot, preferred_element_type=jnp.float32)
        * inverse
    )
    allowed = (places[:, None] >= places[None, :])[None, :, :] & inside[:, None, :]
    logits = jnp.where(allowed[:, None, None, :, :], logits, -1e30)
    peak = jnp.max(logits, axis=-1, keepdims=True)
    raised = jnp.exp(logits - peak)
    attn_prob = raised / jnp.sum(raised, axis=-1, keepdims=True)
    grad_prob = jnp.einsum(
        "eskgh,etkh->ekgst", grad_out, values, preferred_element_type=jnp.float32
    )
    row_total = jnp.sum(attn_prob * grad_prob, axis=-1, keepdims=True)
    grad_logit = (attn_prob * (grad_prob - row_total)).astype(jnp.bfloat16)
    grad_key = (
        jnp.einsum("ekgst,eskgh->etkh", grad_logit, queries, preferred_element_type=jnp.float32)
        * inverse
    )
    grad_key = grad_key * cosine[None, :, None, :] + swap_halves(
        grad_key * sine_tab[None, :, None, :]
    )
    grad_key = grad_key.astype(jnp.bfloat16).reshape(count * SEQ, KV_HEADS * HEAD)
    left_fac = jnp.dot(grad_key, proj_out, preferred_element_type=jnp.float32).reshape(
        count, SEQ, PROJ
    )
    right_fac = jnp.dot(normed, proj_in, preferred_element_type=jnp.float32).reshape(
        count, SEQ, PROJ
    )
    features = jnp.einsum("eti,etj->eij", left_fac, right_fac, precision=lax.Precision.HIGHEST)
    return features.reshape(count, PROJ * PROJ)


HIGHEST = lax.Precision.HIGHEST
CONTRACT_LAST = (((1,), (1,)), ((), ()))


def sweep(system, row, col, k, lanes, subs):
    pivot = 1.0 / jnp.sum(jnp.where(lanes[:1] == k, row, 0.0), axis=1, keepdims=True)
    row = jnp.where(lanes[:1] == k, pivot, row * pivot)
    col = jnp.where(subs[:, :1] == k, -1.0, col)
    return jnp.where((lanes == k) | (subs == k), 0.0, system) - col * row


def score_kernel(feat_ref, test_ref, out_ref, inv_ref):
    count = feat_ref.shape[0]
    width = feat_ref.shape[1]
    mine = out_ref.shape[0]
    first = (lax.axis_index("blk") * lax.axis_size("fsdp") + lax.axis_index("fsdp")) * mine
    feats = feat_ref[...]
    gram = lax.dot_general(
        feats, feats, CONTRACT_LAST, precision=HIGHEST, preferred_element_type=jnp.float32
    )
    lanes = lax.broadcasted_iota(jnp.int32, (count, count), 1)
    subs = lax.broadcasted_iota(jnp.int32, (count, count), 0)
    diagonal = lanes == subs
    mean_diag = jnp.sum(jnp.where(diagonal, gram, 0.0), keepdims=True) / width + 1e-06
    system = gram / mean_diag + jnp.where(diagonal, damping, 0.0)
    if count <= 128:
        for k in range(count):
            system = sweep(system, system[k : k + 1, :], system[:, k : k + 1], k, lanes, subs)
        inv_ref[...] = system
    else:
        inv_ref[...] = system

        def step(k, carry):
            now = inv_ref[...]
            col = jnp.sum(jnp.where(lanes == k, now, 0.0), axis=1, keepdims=True)
            inv_ref[...] = sweep(now, inv_ref[pl.ds(k, 1), :], col, k, lanes, subs)
            return carry

        lax.fori_loop(0, count, step, 0)
    chosen = lax.broadcasted_iota(jnp.int32, (mine, count), 1) == (
        lax.broadcasted_iota(jnp.int32, (mine, count), 0) + first
    )
    rows = lax.dot_general(
        chosen.astype(jnp.float32),
        inv_ref[...],
        (((1,), (0,)), ((), ())),
        precision=HIGHEST,
        preferred_element_type=jnp.float32,
    )
    weighted = jnp.dot(rows, feats, precision=HIGHEST, preferred_element_type=jnp.float32)
    total = None
    for _ in range(3):
        piece = weighted.astype(jnp.bfloat16)
        weighted = weighted - piece.astype(jnp.float32)
        term = lax.dot_general(
            piece, test_ref[...], CONTRACT_LAST, preferred_element_type=jnp.float32
        )
        total = term if total is None else total + term
    out_ref[...] = total


def score(every_feat, tests, mine):
    count = every_feat.shape[0]
    return pl.pallas_call(
        score_kernel,
        out_shape=jax.ShapeDtypeStruct((mine, tests.shape[0]), jnp.float32),
        in_specs=[pl.BlockSpec(memory_space=pltpu.VMEM)] * 2,
        out_specs=pl.BlockSpec(memory_space=pltpu.VMEM),
        scratch_shapes=[pltpu.VMEM((count, count), jnp.float32)],
        compiler_params=pltpu.CompilerParams(vmem_limit_bytes=48 * 1024 * 1024),
    )(every_feat, tests)


def on_device(
    hidden, query, out_grad, lengths, gain, w_key, w_value, proj_in, proj_out, test_feats
):
    normed = normalize(hidden, gain)
    keys_raw = jnp.dot(
        normed,
        lax.all_gather(w_key, "fsdp", axis=0, tiled=True),
        preferred_element_type=jnp.float32,
    )
    values_raw = jnp.dot(
        normed,
        lax.all_gather(w_value, "fsdp", axis=0, tiled=True),
        preferred_element_type=jnp.float32,
    )
    features = features_of(
        normed, keys_raw, values_raw, query, out_grad, lengths, proj_in, proj_out
    )
    every_feat = lax.all_gather(features, ("blk", "fsdp"), axis=0, tiled=True)
    tests = lax.all_gather(test_feats, "blk", axis=0, tiled=True)
    return score(every_feat, tests, features.shape[0])


def solution(mesh):
    in_specs = (
        P(("groups", "blk", "fsdp"), None),
        P(("groups", "blk", "fsdp"), None),
        P(("groups", "blk", "fsdp"), None),
        P(("groups", "blk", "fsdp")),
        P(),
        P("fsdp", None),
        P("fsdp", None),
        P(),
        P(),
        P("blk", None),
    )
    out_specs = P(("groups", "blk", "fsdp"), None)
    return jax.shard_map(
        on_device, mesh=mesh, in_specs=in_specs, out_specs=out_specs, check_vma=False
    )
```

profile of v0, /device:TPU:1, one launch (start us, length us, event | category | flops | bytes accessed | tf_op | source)
XLA Modules:
  0.0 185.1 jit_solution(9044342371690048925)
XLA Ops:
  6.5 0.7 all-gather.5.cloned.1.call-update
  7.3 0.7 all-gather.7.cloned.1.call-update
  8.1 0.7 all-gather.9.cloned.1.call-update
  8.8 0.5 fusion.1
  9.3 3.2 %reshape.95 = bf16[4,64,8,4,128]{4,3,2,1,0:T(4,128)(2,1)S(1)} reshape(bf16[256,4096]{1,0:T(8,128)(2,1)} %param.11) | data formatting | bytes 4194304 | tf_op jit(solution)/shard_map/reshape | solution.py:51
  12.7 4.4 %reshape.96 = bf16[4,64,8,4,128]{4,3,2,1,0:T(4,128)(2,1)} reshape(bf16[256,4096]{1,0:T(8,128)(2,1)} %param.12) | data formatting | bytes 4194304 | tf_op jit(solution)/shard_map/reshape | solution.py:56
  17.1 2.6 %fusion.47 = f32[256,32]{0,1:T(8,128)S(1)} fusion(bf16[4096,32]{0,1:T(8,128)(2,1)S(1)} %copy-done, bf16[256,4096]{1,0:T(8,128)(2,1)} %param.10, f32[4096]{0:T(1024)S(1)} %copy-done.10, f32[256]{0:T(256)S(1)} %add_rsqrt_fusion), kind=kOutput, calls=%fused_computation.67 | convolution fusion | flops 71303168 | bytes 2409472 | tf_op jit(solution)/shard_map/dot_general | solution.py:85
  20.0 0.7 broadcast_and_fusion
  20.7 0.7 broadcast_multiply_fusion
  21.5 48.3 %all-gather.5.cloned.1.call-done = bf16[4096,1024]{1,0:T(8,128)(2,1)} async-done(((bf16[1024,1024]{1,0:T(8,128)(2,1)}), bf16[4096,1024]{1,0:T(8,128)(2,1)}) %all-gather.5.cloned.1.call-update) | async-done | bytes 8388624 | tf_op jit(solution)/shard_map/all_gather | solution.py:171
  69.7 6.4 %convolution_bitcast_fusion = f32[32,8,8,128]{3,1,2,0:T(8,128)S(1)} fusion(bf16[4096,1024]{1,0:T(8,128)(2,1)} %all-gather.5.cloned.1.call-done, bf16[256,4096]{1,0:T(8,128)(2,1)} %param.10, f32[4096]{0:T(1024)S(1)} %copy-done.10, f32[256]{0:T(256)S(1)} %add_rsqrt_fusion), kind=kOutput, calls=%fused_computation.27 | convolution fusion | flops 2151677952 | bytes 11551744 | tf_op jit(solution)/shard_map/dot_general | solution.py:169
  76.7 1.3 copy.65
  78.0 1.2 copy.66
  79.1 50.5 %all-gather.7.cloned.1.call-done = bf16[4096,1024]{1,0:T(8,128)(2,1)} async-done(((bf16[1024,1024]{1,0:T(8,128)(2,1)}), bf16[4096,1024]{1,0:T(8,128)(2,1)}) %all-gather.7.cloned.1.call-update) | async-done | bytes 8388624 | tf_op jit(solution)/shard_map/all_gather | solution.py:176
  129.6 6.6 %fusion.24 = bf16[32,8,8,128]{3,1,2,0:T(8,128)(2,1)S(1)} fusion(bf16[4096,1024]{1,0:T(8,128)(2,1)} %all-gather.7.cloned.1.call-done, bf16[256,4096]{1,0:T(8,128)(2,1)} %param.10, f32[4096]{0:T(1024)} %param.14, f32[256]{0:T(256)S(1)} %add_rsqrt_fusion), kind=kOutput, calls=%fused_computation.29 | convolution fusion | flops 2151940096 | bytes 11027456 | tf_op jit(solution)/shard_map/dot_general | solution.py:174
  136.4 2.1 %fusion.17 = f32[4,8,64,64,4]{3,2,4,1,0:T(8,128)S(1)} fusion(bf16[4,64,8,4,128]{4,3,2,1,0:T(4,128)(2,1)S(1)} %reshape.95, f32[4,64,8,64]{3,1,2,0:T(8,128)S(1)} %copy-done.2, f32[4,64,8,64]{3,1,2,0:T(8,128)S(1)} %copy-done.3, f32[64,128]{1,0:T(8,128)S(1)} %copy-done.6, f32[64,128]{1,0:T(8,128)S(1)} %copy-done.7, f32[4,64,8,128]{3,2,1,0:T(8,128)S(1)} %bitcast.68), kind=kOutput, calls=%fused_computation.24 | convolution fusion | flops 135528448 | bytes 6356992 | tf_op jit(solution)/shard_map/eskgh,etkh->ekgst/dot_general | solution.py:61
  138.6 1.4 fusion.53
  140.2 2.5 %fusion.4 = (f32[4,8,4,64]{3,2,1,0:T(4,128)S(1)}, f32[4,8,64,64,4]{3,2,4,1,0:T(8,128)S(1)}) fusion(f32[4,8,4,64,64]{3,4,2,1,0:T(8,128)S(1)} %get-tuple-element.17, f32[4,8,4,64]{3,2,1,0:T(4,128)S(1)} %get-tuple-element.16, bf16[4,64,8,4,128]{4,3,2,1,0:T(4,128)(2,1)S(1)} %copy-done.5, pred[4,64]{1,0:T(4,128)(4,1)S(1)} %iota_compare_fusion.1, ...), kind=kOutput, calls=%fused_computation.8 | convolution fusion | flops 136830976 | bytes 6881536 | tf_op jit(solution)/shard_map/eskgh,etkh->ekgst/dot_general | solution.py:69
  142.7 1.9 %fusion.19 = f32[4,8,64,128]{3,2,1,0:T(8,128)S(1)} fusion(bf16[4,64,8,4,128]{4,3,2,1,0:T(4,128)(2,1)S(1)} %reshape.95, f32[4,8,64,64,4]{3,2,4,1,0:T(8,128)S(1)} %get-tuple-element.19, f32[4,8,4,64]{3,2,1,0:T(4,128)S(1)} %get-tuple-element.18, f32[4,8,4,64,64]{3,4,2,1,0:T(8,128)S(1)} %get-tuple-element.17, f32[4,8,4,64]{3,2,1,0:T(4,128)S(1)} %get-tuple-element.16), kind=kOutput, calls=%fused_computation.26 | convolution fusion | flops 136314880 | bytes 7405568 | tf_op jit(solution)/shard_map/ekgst,eskgh->etkh/dot_general | solution.py:75
  145.2 0.4 copy-done.8
  145.5 0.5 fusion.32
  146.4 22.1 %all-gather = f32[16,4,1024]{2,1,0:T(4,128)S(1)} all-gather(f32[1,4,1024]{2,1,0:T(4,128)S(1)} %reshape.99), channel_id=1, replica_groups=mesh['groups'=2,'blk'=4,'fsdp'=4] {'blk','fsdp'}, dimensions={0}, use_global_device_ids=true | all-gather | bytes 278528 | tf_op jit(solution)/shard_map/all_gather | solution.py:182
  168.6 1.2 copy-done.1
  169.8 8.7 %shard_map.100 = f32[4,512]{1,0:T(4,128)} custom-call(f32[64,1024]{1,0:T(8,128)S(1)} %reshape.100.feat_ref, bf16[512,1024]{1,0:T(8,128)(2,1)S(1)} %copy-done.1), custom_call_target="tpu_custom_call" | custom-call | tf_op jit(solution)/shard_map/pallas_call | solution.py:155
  (42 shorter events, 2.3 us)
Async XLA Ops:
  6.5 10.5 %copy-start = (bf16[4096,32]{0,1:T(8,128)(2,1)S(1)}, bf16[4096,32]{0,1:T(8,128)(2,1)}, u32[]{:S(2)}) copy-start(bf16[4096,32]{0,1:T(8,128)(2,1)} %param.17) | copy-start | bytes 786436
  6.5 2.3 %copy-start.4 = (bf16[256,4096]{1,0:T(8,128)(2,1)S(1)}, bf16[256,4096]{1,0:T(8,128)(2,1)}, u32[]{:S(2)}) copy-start(bf16[256,4096]{1,0:T(8,128)(2,1)} %param.10) | copy-start | bytes 6291460
  6.5 63.2 %all-gather.5.cloned.1.call-start = ((), (), s32[]{:S(2)}) async-start(), calls=%async_computation | async-start | bytes 10485760 | tf_op jit(solution)/shard_map/all_gather | solution.py:171
  7.3 5.3 %copy-start.11 = (s32[4]{0:T(128)S(1)}, s32[4]{0:T(128)}, u32[]{:S(2)}) copy-start(s32[4]{0:T(128)} %param.13) | copy-start | bytes 52
  7.3 122.4 %all-gather.7.cloned.1.call-start = ((), (), s32[]{:S(2)}) async-start(), calls=%async_computation.1 | async-start | bytes 10485760 | tf_op jit(solution)/shard_map/all_gather | solution.py:176
  8.0 160.6 %all-gather.9.cloned.1.call-start = ((), (), s32[]{:S(2)}) async-start(), calls=%async_computation.2 | async-start | bytes 1310720 | tf_op jit(solution)/shard_map/all_gather | solution.py:183
  9.3 7.8 %copy-start.10 = (f32[4096]{0:T(1024)S(1)}, f32[4096]{0:T(1024)}, u32[]{:S(2)}) copy-start(f32[4096]{0:T(1024)} %param.14) | copy-start | bytes 49156
  129.6 6.7 %copy-start.2 = (f32[4,64,8,64]{3,1,2,0:T(8,128)S(1)}, f32[4,64,8,64]{3,1,2,0:T(8,128)}, u32[]{:S(2)}) copy-start(f32[4,64,8,64]{3,1,2,0:T(8,128)} %copy.65) | copy-start | bytes 1572868
  129.6 6.7 %copy-start.3 = (f32[4,64,8,64]{3,1,2,0:T(8,128)S(1)}, f32[4,64,8,64]{3,1,2,0:T(8,128)}, u32[]{:S(2)}) copy-start(f32[4,64,8,64]{3,1,2,0:T(8,128)} %copy.66) | copy-start | bytes 1572868
  129.6 6.7 %copy-start.6 = (f32[64,128]{1,0:T(8,128)S(1)}, f32[64,128]{1,0:T(8,128)}, u32[]{:S(2)}) copy-start(f32[64,128]{1,0:T(8,128)} %get-tuple-element.6) | copy-start | bytes 98308
  129.6 6.7 %copy-start.7 = (f32[64,128]{1,0:T(8,128)S(1)}, f32[64,128]{1,0:T(8,128)}, u32[]{:S(2)}) copy-start(f32[64,128]{1,0:T(8,128)} %get-tuple-element.20) | copy-start | bytes 98308
  136.4 2.2 %copy-start.9 = (pred[4,64,64]{1,2,0:T(8,128)(4,1)S(1)}, pred[4,64,64]{1,2,0:T(8,128)(4,1)}, u32[]{:S(2)}) copy-start(pred[4,64,64]{1,2,0:T(8,128)(4,1)} %broadcast_and_fusion) | copy-start | bytes 49156
  138.5 1.7 copy-start.5
  144.7 0.8 copy-start.8
  168.6 1.2 copy-start.1
Sparse Core Ops, SparseCore 0:
  8.9 60.7 all-gather.4
  71.3 58.2 all-gather.6
  131.2 28.2 all-gather.8
where the time goes:
time: 186 us; the launch traced here: 185 us
  waiting for transfers between devices  101 us (54%)
  matrix products  22.9 us (12%)
  blocking collectives  22.1 us (12%)
  between operations  13.4 us (7%)
  local copies, waits for them, and re-layouts  13.3 us (7%)
  Pallas kernels  8.75 us (5%)
  other arithmetic  3.7 us (2%)
    all_gather x1, waiting for transfers between devices, on_device(): lax.all_gather(w_value, 'fsdp', axis=0, tiled=True)  50.5 us
    all_gather x1, waiting for transfers between devices, on_device(): lax.all_gather(w_key, 'fsdp', axis=0, tiled=True)  48.3 us
    all_gather x1, blocking collectives, on_device(): every_feat = lax.all_gather(features, ('blk', 'fsdp'), axis=0, tiled=True)  22.1 us
    pallas_call x1, Pallas kernels, score(): pl.pallas_call(score_kernel, out_shape=jax.ShapeDtypeStruct((mine, tests....  8.75 us
    dot_general x1, matrix products, on_device(): jnp.dot(normed, lax.all_gather(w_value, 'fsdp', axis=0, tiled=True), pref...  6.56 us
    dot_general x1, matrix products, on_device(): jnp.dot(normed, lax.all_gather(w_key, 'fsdp', axis=0, tiled=True), prefer...  6.4 us
    unnamed x30, local copies, waits for them, and re-layouts  4.77 us
    reshape x1, local copies, waits for them, and re-layouts, features_of(): out_grad.reshape(count, SEQ, KV_HEADS, group_size, HEAD)  4.43 us
  transfers between devices with their start and end apart: 3, of which 2 were waited for; matrix products, arithmetic and copies ran while one was open for 21% of the time, Pallas kernels for 0%

commit v1 on v0

v1 whole, which is shorter than its diff:
```python
import math

import jax
import jax.numpy as jnp
import numpy as np
from jax import lax
from jax.experimental import pallas as pl
from jax.experimental.pallas import tpu as pltpu
from jax.sharding import PartitionSpec as P

HEADS = 32
KV_HEADS = 8
HEAD = 128
PROJ = 32
SEQ = 64


norm_eps = 1e-05
rope_base = 500000.0
damping = 0.01
GROUP = HEADS // KV_HEADS
AHEAD = 2


def rope_tables(count):
    freqs = rope_base ** (-2.0 * np.arange(HEAD // 2) / HEAD)
    angles = np.arange(SEQ)[:, None] * freqs[None, :]
    cosine, sine = np.cos(angles), np.sin(angles)
    cosine = np.concatenate([cosine, cosine], -1)
    sine = np.concatenate([-sine, sine], -1)
    return [np.tile(table, (count, 1)).astype(np.float32) for table in (cosine, sine)]


HIGHEST = lax.Precision.HIGHEST
CONTRACT_LAST = (((1,), (1,)), ((), ()))


def sweep(system, row, col, k, lanes, subs):
    pivot = 1.0 / jnp.sum(jnp.where(lanes[:1] == k, row, 0.0), axis=1, keepdims=True)
    row = jnp.where(lanes[:1] == k, pivot, row * pivot)
    col = jnp.where(subs[:, :1] == k, -1.0, col)
    return jnp.where((lanes == k) | (subs == k), 0.0, system) - col * row


def score_kernel(feat_ref, test_ref, out_ref, inv_ref):
    count = feat_ref.shape[0]
    width = feat_ref.shape[1]
    mine = out_ref.shape[0]
    first = (lax.axis_index("blk") * lax.axis_size("fsdp") + lax.axis_index("fsdp")) * mine
    feats = feat_ref[...]
    gram = lax.dot_general(
        feats, feats, CONTRACT_LAST, precision=HIGHEST, preferred_element_type=jnp.float32
    )
    lanes = lax.broadcasted_iota(jnp.int32, (count, count), 1)
    subs = lax.broadcasted_iota(jnp.int32, (count, count), 0)
    diagonal = lanes == subs
    mean_diag = jnp.sum(jnp.where(diagonal, gram, 0.0), keepdims=True) / width + 1e-06
    system = gram / mean_diag + jnp.where(diagonal, damping, 0.0)
    if count <= 128:
        for k in range(count):
            system = sweep(system, system[k : k + 1, :], system[:, k : k + 1], k, lanes, subs)
        inv_ref[...] = system
    else:
        inv_ref[...] = system

        def step(k, carry):
            now = inv_ref[...]
            col = jnp.sum(jnp.where(lanes == k, now, 0.0), axis=1, keepdims=True)
            inv_ref[...] = sweep(now, inv_ref[pl.ds(k, 1), :], col, k, lanes, subs)
            return carry

        lax.fori_loop(0, count, step, 0)
    chosen = lax.broadcasted_iota(jnp.int32, (mine, count), 1) == (
        lax.broadcasted_iota(jnp.int32, (mine, count), 0) + first
    )
    rows = lax.dot_general(
        chosen.astype(jnp.float32),
        inv_ref[...],
        (((1,), (0,)), ((), ())),
        precision=HIGHEST,
        preferred_element_type=jnp.float32,
    )
    weighted = jnp.dot(rows, feats, precision=HIGHEST, preferred_element_type=jnp.float32)
    total = None
    for _ in range(3):
        piece = weighted.astype(jnp.bfloat16)
        weighted = weighted - piece.astype(jnp.float32)
        term = lax.dot_general(
            piece, test_ref[...], CONTRACT_LAST, preferred_element_type=jnp.float32
        )
        total = term if total is None else total + term
    out_ref[...] = total


def score(every_feat, tests, mine):
    count = every_feat.shape[0]
    return pl.pallas_call(
        score_kernel,
        out_shape=jax.ShapeDtypeStruct((mine, tests.shape[0]), jnp.float32),
        in_specs=[pl.BlockSpec(memory_space=pltpu.VMEM)] * 2,
        out_specs=pl.BlockSpec(memory_space=pltpu.VMEM),
        scratch_shapes=[pltpu.VMEM((count, count), jnp.float32)],
        compiler_params=pltpu.CompilerParams(vmem_limit_bytes=48 * 1024 * 1024),
    )(every_feat, tests)


def feature_kernel(
    hidden_ref, query_ref, outg_ref, keep_ref, gain_ref, wk_ref, wv_ref, pin_ref, pout_ref,
    cos_ref, sin_ref, out_ref,
    wbuf, hid, que, outg, normed, left, right,
    in_sem, own_sem, sib_send, sib_recv, x_send, x_recv, y_send, y_recv,
    fx_send, fx_recv, fy_send, fy_recv,
):
    count = out_ref.shape[0]
    rows = wk_ref.shape[0]
    half_rows = rows // 2
    inverse = 1.0 / math.sqrt(HEAD)
    g = lax.axis_index("groups")
    f = lax.axis_index("fsdp")
    sib = f + 1 - 2 * (f % 2)
    across = (f + 2) % 4
    beyond = (sib + 2) % 4
    other = g + 1 - 2 * (g % 2)
    half = g % 2

    def rows_of(owner, part):
        return pl.ds(pl.multiple_of(owner * rows + part * half_rows, half_rows), half_rows)

    def copy(h, where, send, recv, to):
        part = wbuf.at[h, :, where, :]
        return pltpu.make_async_remote_copy(
            src_ref=part, dst_ref=part, send_sem=send.at[h], recv_sem=recv.at[h],
            device_id=to, device_id_type=pl.DeviceIdType.MESH,
        )

    whole_own = pl.ds(pl.multiple_of(f * rows, rows), rows)
    whole_sib = pl.ds(pl.multiple_of(sib * rows, rows), rows)
    to_sib, to_across, to_other = {"fsdp": sib}, {"fsdp": across}, {"groups": other}

    def own(h, kind):
        return pltpu.make_async_copy(
            (wk_ref, wv_ref)[kind].at[:, pl.ds(pl.multiple_of(h * HEAD, HEAD), HEAD)],
            wbuf.at[h, kind, whole_own, :],
            own_sem.at[kind, h],
        )

    def send_own(h):
        own(h, 0).wait()
        own(h, 1).wait()
        copy(h, rows_of(f, half), x_send, x_recv, to_across).start()
        copy(h, whole_own, sib_send, sib_recv, to_sib).start()

    def start_own(h, carry):
        own(h, 0).start()
        own(h, 1).start()
        return carry

    lax.fori_loop(0, KV_HEADS, start_own, 0)
    loads = [
        pltpu.make_async_copy(src, dst, in_sem.at[i])
        for i, (src, dst) in enumerate(((hidden_ref, hid), (query_ref, que), (outg_ref, outg)))
    ]
    for load in loads:
        load.start()

    barrier = pltpu.get_barrier_semaphore()
    for to in (to_sib, to_across, to_other):
        pl.semaphore_signal(barrier, inc=1, device_id=to, device_id_type=pl.DeviceIdType.MESH)
    pl.semaphore_wait(barrier, 3)
    for h in range(AHEAD):
        send_own(h)

    loads[0].wait()
    strip = 16

    def normalize(i, carry):
        where = pl.ds(pl.multiple_of(i * strip, strip), strip)
        widened = hid[where, :].astype(jnp.float32)
        scale = lax.rsqrt(jnp.mean(widened * widened, axis=1, keepdims=True) + norm_eps)
        normed[where, :] = (widened * scale * gain_ref[...]).astype(jnp.bfloat16)
        return carry

    lax.fori_loop(0, hid.shape[0] // strip, normalize, 0)
    right[...] = jnp.dot(normed[...], pin_ref[...], preferred_element_type=jnp.float32)
    left[...] = jnp.zeros_like(left)
    loads[1].wait()
    loads[2].wait()

    def stack(ref, e, h):
        block = ref[e * SEQ : (e + 1) * SEQ, pl.ds(pl.multiple_of(h * GROUP * HEAD, HEAD), GROUP * HEAD)]
        return jnp.concatenate([block[:, i * HEAD : (i + 1) * HEAD] for i in range(GROUP)], axis=0)

    def head(h):
        weights = jnp.concatenate([wbuf[h, 0], wbuf[h, 1]], axis=1)
        both = jnp.dot(normed[...], weights, preferred_element_type=jnp.float32)
        cosine, sine = cos_ref[...], sin_ref[...]
        keys = both[:, :HEAD]
        keys = (keys * cosine + pltpu.roll(keys, HEAD // 2, 1) * sine).astype(jnp.bfloat16)
        values = both[:, HEAD:].astype(jnp.bfloat16)
        causal = lax.broadcasted_iota(jnp.int32, (SEQ, GROUP * SEQ), 0) <= (
            lax.broadcasted_iota(jnp.int32, (SEQ, GROUP * SEQ), 1) % SEQ
        )
        grads = []
        for e in range(count):
            mine = slice(e * SEQ, (e + 1) * SEQ)
            queries = stack(que, e, h)
            logits = lax.dot_general(
                keys[mine], queries, CONTRACT_LAST, preferred_element_type=jnp.float32
            ) * inverse
            logits = jnp.where(causal, logits, -1e30)
            raised = jnp.exp(logits - jnp.max(logits, axis=0, keepdims=True))
            prob = raised / jnp.sum(raised, axis=0, keepdims=True)
            grad_prob = lax.dot_general(
                values[mine], stack(outg, e, h), CONTRACT_LAST, preferred_element_type=jnp.float32
            ) * keep_ref[e : e + 1, :]
            total = jnp.sum(prob * grad_prob, axis=0, keepdims=True)
            grad_logit = (prob * (grad_prob - total)).astype(jnp.bfloat16)
            grads.append(jnp.dot(grad_logit, queries, preferred_element_type=jnp.float32))
        grad = jnp.concatenate(grads, axis=0) * inverse
        grad = grad * cosine + pltpu.roll(grad * sine, HEAD // 2, 1)
        block = pout_ref[pl.ds(pl.multiple_of(h * HEAD, HEAD), HEAD), :]
        left[...] += jnp.dot(grad.astype(jnp.bfloat16), block, preferred_element_type=jnp.float32)

    def step(i, carry):
        @pl.when(i < KV_HEADS)
        def _():
            copy(i, rows_of(across, half), x_send, x_recv, to_across).wait_recv()
            copy(i, rows_of(across, half), y_send, y_recv, to_other).start()
            copy(i, rows_of(across, half), fx_send, fx_recv, to_sib).start()

        @pl.when(i + AHEAD < KV_HEADS)
        def _():
            send_own(i + AHEAD)

        @pl.when((i >= 1) & (i <= KV_HEADS))
        def _():
            copy(i - 1, rows_of(across, 1 - half), y_send, y_recv, to_other).wait_recv()
            copy(i - 1, rows_of(across, 1 - half), fy_send, fy_recv, to_sib).start()

        @pl.when(i >= 2)
        def _():
            h = i - 2
            copy(h, whole_sib, sib_send, sib_recv, to_sib).wait_recv()
            copy(h, rows_of(beyond, half), fx_send, fx_recv, to_sib).wait_recv()
            copy(h, rows_of(beyond, 1 - half), fy_send, fy_recv, to_sib).wait_recv()
            head(h)

        return carry

    lax.fori_loop(0, KV_HEADS + 2, step, 0)

    def finish(h, carry):
        copy(h, rows_of(f, half), x_send, x_recv, to_across).wait_send()
        copy(h, whole_own, sib_send, sib_recv, to_sib).wait_send()
        copy(h, rows_of(across, half), y_send, y_recv, to_other).wait_send()
        copy(h, rows_of(across, half), fx_send, fx_recv, to_sib).wait_send()
        copy(h, rows_of(across, 1 - half), fy_send, fy_recv, to_sib).wait_send()
        return carry

    lax.fori_loop(0, KV_HEADS, finish, 0)
    shape = left.shape
    belongs = lax.broadcasted_iota(jnp.int32, shape, 0) // SEQ == (
        lax.broadcasted_iota(jnp.int32, shape, 1) % count
    )
    outer = lax.dot_general(
        jnp.where(belongs, left[...], 0.0),
        right[...],
        (((0,), (0,)), ((), ())),
        precision=HIGHEST,
        preferred_element_type=jnp.float32,
    )
    for i in range(PROJ):
        out_ref[:, i * PROJ : (i + 1) * PROJ] = outer[i * count : (i + 1) * count, :]


def features_of(hidden, query, out_grad, lengths, gain, w_key, w_value, proj_in, proj_out):
    count = lengths.shape[0]
    tokens, width = hidden.shape
    keep = (jnp.arange(SEQ)[None, :] < lengths[:, None]).astype(jnp.float32)
    cosine, sine = rope_tables(count)
    anywhere = pl.BlockSpec(memory_space=pl.ANY)
    vmem = pl.BlockSpec(memory_space=pltpu.VMEM)
    heads = pltpu.SemaphoreType.DMA((KV_HEADS,))
    return pl.pallas_call(
        feature_kernel,
        out_shape=jax.ShapeDtypeStruct((count, PROJ * PROJ), jnp.float32),
        in_specs=[anywhere] * 3 + [vmem] * 2 + [anywhere] * 2 + [vmem] * 4,
        out_specs=vmem,
        scratch_shapes=[
            pltpu.VMEM((KV_HEADS, 2, width, HEAD), jnp.bfloat16),
            pltpu.VMEM((tokens, width), jnp.bfloat16),
            pltpu.VMEM((tokens, query.shape[1]), jnp.bfloat16),
            pltpu.VMEM((tokens, query.shape[1]), jnp.bfloat16),
            pltpu.VMEM((tokens, width), jnp.bfloat16),
            pltpu.VMEM((tokens, PROJ * count), jnp.float32),
            pltpu.VMEM((tokens, PROJ), jnp.float32),
            pltpu.SemaphoreType.DMA((3,)),
            pltpu.SemaphoreType.DMA((2, KV_HEADS)),
        ]
        + [heads] * 10,
        compiler_params=pltpu.CompilerParams(
            collective_id=0, has_side_effects=True, vmem_limit_bytes=56 * 1024 * 1024
        ),
        cost_estimate=pl.CostEstimate(
            flops=2 * tokens * width * 2 * KV_HEADS * HEAD, bytes_accessed=100_000_000, transcendentals=0
        ),
    )(
        hidden, query, out_grad, jnp.tile(keep, (1, GROUP)), gain.reshape(1, width), w_key, w_value,
        proj_in, jnp.repeat(proj_out, count, axis=1), cosine, sine,
    )


def on_device(
    hidden, query, out_grad, lengths, gain, w_key, w_value, proj_in, proj_out, test_feats
):
    features = features_of(
        hidden, query, out_grad, lengths, gain, w_key, w_value, proj_in, proj_out
    )
    every_feat = lax.all_gather(features, ("blk", "fsdp"), axis=0, tiled=True)
    tests = lax.all_gather(test_feats, "blk", axis=0, tiled=True)
    return score(every_feat, tests, features.shape[0])


def solution(mesh):
    in_specs = (
        P(("groups", "blk", "fsdp"), None),
        P(("groups", "blk", "fsdp"), None),
        P(("groups", "blk", "fsdp"), None),
        P(("groups", "blk", "fsdp")),
        P(),
        P("fsdp", None),
        P("fsdp", None),
        P(),
        P(),
        P("blk", None),
    )
    out_specs = P(("groups", "blk", "fsdp"), None)
    return jax.shard_map(
        on_device, mesh=mesh, in_specs=in_specs, out_specs=out_specs, check_vma=False
    )
```

time: 186 us -> 115 us (0.62)
  waiting for transfers between devices: 101 us -> 0.73 us
  Pallas kernels: 8.75 us -> 72.2 us
  matrix products: 22.9 us -> 0 us
  local copies, waits for them, and re-layouts: 13.3 us -> 6.12 us
  other arithmetic: 3.7 us -> 0.07 us
    all_gather x2 -> x0, waiting for transfers between devices: 98.8 us -> none  [the longest x1 50.5 us: on_device(): lax.all_gather(w_value, 'fsdp', axis=0, tiled=True)]
    pallas_call x0 -> x1, Pallas kernels: none -> 63.4 us  [features_of(): pl.pallas_call(feature_kernel, out_shape=jax.ShapeDtypeStruct((count, PRO...]
    dot_general x8 -> x0, matrix products: 22.9 us -> none  [the longest x1 6.56 us: on_device(): jnp.dot(normed, lax.all_gather(w_value, 'fsdp', axis=0, tiled=True), pref...]
    reshape x3 -> x2, local copies, waits for them, and re-layouts: 7.78 us -> 0.91 us  [features_of(): jnp.repeat(proj_out, count, axis=1)]
    unnamed x30 -> x6, local copies, waits for them, and re-layouts: 4.77 us -> 3.62 us
  transfers between devices with their start and end apart: 3 -> 1, of which waited for: 2 -> 0; matrix products, arithmetic and copies ran while one was open for 21% -> 4% of each run, Pallas kernels for 0% -> 55%
where the time goes in v1:
time: 115 us
  Pallas kernels  72.2 us (63%)
  blocking collectives  22.4 us (19%)
  between operations  13.4 us (12%)
  local copies, waits for them, and re-layouts  6.12 us (5%)
    pallas_call x1, Pallas kernels, features_of(): pl.pallas_call(feature_kernel, out_shape=jax.ShapeDtypeStruct((count, PRO...  63.4 us
    all_gather x1, blocking collectives, on_device(): every_feat = lax.all_gather(features, ('blk', 'fsdp'), axis=0, tiled=True)  22.4 us
    pallas_call x1, Pallas kernels, score(): pl.pallas_call(score_kernel, out_shape=jax.ShapeDtypeStruct((mine, tests....  8.75 us
    unnamed x6, local copies, waits for them, and re-layouts  3.62 us
  transfers between devices with their start and end apart: 1, of which 0 were waited for; matrix products, arithmetic and copies ran while one was open for 4% of the time, Pallas kernels for 55%

profile of v1, /device:TPU:1, one launch (start us, length us, event | category | flops | bytes accessed | tf_op | source)
XLA Modules:
  0.0 114.9 jit_solution(9030515052903020862)
XLA Ops:
  6.5 0.0 copy-start.1
  6.5 0.0 all-gather.3.cloned.1.call-start
  6.5 0.7 all-gather.3.cloned.1.call-update
  7.3 2.3 %copy.17.pin_ref = bf16[4096,32]{1,0:T(8,128)(2,1)} copy(bf16[4096,32]{0,1:T(8,128)(2,1)} %param.19) | data formatting | bytes 524288 | tf_op args[7]
  9.6 0.9 broadcast_in_dim.2
  10.5 0.1 reshape.29
  10.6 0.8 copy.18.pout_ref
  11.4 0.0 copy-done.1
  11.4 0.1 fusion
  11.5 0.7 tile.10.keep_ref
  12.2 63.4 %shard_map.118 = f32[4,1024]{1,0:T(4,128)} custom-call(bf16[256,4096]{1,0:T(8,128)(2,1)} %hidden_ref.1, bf16[256,4096]{1,0:T(8,128)(2,1)} %query_ref.1, bf16[256,4096]{1,0:T(8,128)(2,1)} %outg_ref.1, f32[4,256]{1,0:T(4,128)} %tile.10.keep_ref, f32[1,4096]{1,0:T(1,128)} %bitcast.5, bf16[1024,1024]{1,0:T(8,128)(2,1)} %wk_ref.1, bf16[1024,1024]{1,0:T(8,128)(2,1)} %wv_ref.1, ...), custom_call_target="tpu_custom_call" | custom-call | flops 4294967296 | bytes 100000000 | tf_op jit(solution)/shard_map/pallas_call | solution.py:284
  75.6 22.4 %all-gather = f32[16,4,1024]{2,1,0:T(4,128)S(1)} all-gather(f32[1,4,1024]{2,1,0:T(4,128)} %bitcast.4), channel_id=1, replica_groups=mesh['groups'=2,'blk'=4,'fsdp'=4] {'blk','fsdp'}, dimensions={0}, use_global_device_ids=true | all-gather | bytes 278528 | tf_op jit(solution)/shard_map/all_gather | solution.py:319
  98.0 0.1 reshape.31.feat_ref
  98.1 0.0 all-gather.3.cloned.1.call-done.test_ref
  98.1 0.0 copy-start
  98.1 1.2 %copy-done = bf16[512,1024]{1,0:T(8,128)(2,1)S(1)} copy-done((bf16[512,1024]{1,0:T(8,128)(2,1)S(1)}, bf16[512,1024]{1,0:T(8,128)(2,1)}, u32[]{:S(2)}) %copy-start) | copy-done | bytes 1048600
  99.3 8.7 %shard_map.119 = f32[4,512]{1,0:T(4,128)} custom-call(f32[64,1024]{1,0:T(8,128)S(1)} %reshape.31.feat_ref, bf16[512,1024]{1,0:T(8,128)(2,1)S(1)} %copy-done), custom_call_target="tpu_custom_call" | custom-call | tf_op jit(solution)/shard_map/pallas_call | solution.py:97
  (1 shorter events, 0.0 us)
Async XLA Ops:
  6.5 4.9 %copy-start.1 = (s32[4]{0:T(128)S(1)}, s32[4]{0:T(128)}, u32[]{:S(2)}) copy-start(s32[4]{0:T(128)} %param.15) | copy-start | bytes 52
  6.5 91.6 %all-gather.3.cloned.1.call-start = ((), (), s32[]{:S(2)}) async-start(), calls=%async_computation | async-start | bytes 1310720 | tf_op jit(solution)/shard_map/all_gather | solution.py:320
  98.1 1.2 %copy-start = (bf16[512,1024]{1,0:T(8,128)(2,1)S(1)}, bf16[512,1024]{1,0:T(8,128)(2,1)}, u32[]{:S(2)}) copy-start(bf16[512,1024]{1,0:T(8,128)(2,1)} %all-gather.3.cloned.1.call-done.test_ref) | copy-start | bytes 3145732
Sparse Core Ops, SparseCore 0:
  8.9 29.9 all-gather.2

commit v2 on v1

--- a/solution.py
+++ b/solution.py
@@ -42,12 +42,8 @@
     return jnp.where((lanes == k) | (subs == k), 0.0, system) - col * row
 
 
-def score_kernel(feat_ref, test_ref, out_ref, inv_ref):
-    count = feat_ref.shape[0]
-    width = feat_ref.shape[1]
-    mine = out_ref.shape[0]
-    first = (lax.axis_index("blk") * lax.axis_size("fsdp") + lax.axis_index("fsdp")) * mine
-    feats = feat_ref[...]
+def score(feats, tests, inv_ref, first, mine):
+    count, width = feats.shape
     gram = lax.dot_general(
         feats, feats, CONTRACT_LAST, precision=HIGHEST, preferred_element_type=jnp.float32
     )
@@ -86,32 +82,21 @@
         piece = weighted.astype(jnp.bfloat16)
         weighted = weighted - piece.astype(jnp.float32)
         term = lax.dot_general(
-            piece, test_ref[...], CONTRACT_LAST, preferred_element_type=jnp.float32
+            piece, tests, CONTRACT_LAST, preferred_element_type=jnp.float32
         )
         total = term if total is None else total + term
-    out_ref[...] = total
-
-
-def score(every_feat, tests, mine):
-    count = every_feat.shape[0]
-    return pl.pallas_call(
-        score_kernel,
-        out_shape=jax.ShapeDtypeStruct((mine, tests.shape[0]), jnp.float32),
-        in_specs=[pl.BlockSpec(memory_space=pltpu.VMEM)] * 2,
-        out_specs=pl.BlockSpec(memory_space=pltpu.VMEM),
-        scratch_shapes=[pltpu.VMEM((count, count), jnp.float32)],
-        compiler_params=pltpu.CompilerParams(vmem_limit_bytes=48 * 1024 * 1024),
-    )(every_feat, tests)
-
-
-def feature_kernel(
-    hidden_ref, query_ref, outg_ref, keep_ref, gain_ref, wk_ref, wv_ref, pin_ref, pout_ref,
-    cos_ref, sin_ref, out_ref,
-    wbuf, hid, que, outg, normed, left, right,
+    return total
+
+
+def score_kernel(
+    hidden_ref, query_ref, outg_ref, len_ref, gain_ref, wk_ref, wv_ref, pin_ref, pout_ref,
+    test_ref, cos_ref, sin_ref, out_ref,
+    wbuf, hid, que, outg, normed, left, right, fbuf, flat, tests, inv_ref,
     in_sem, own_sem, sib_send, sib_recv, x_send, x_recv, y_send, y_recv,
     fx_send, fx_recv, fy_send, fy_recv,
+    t_sem, t_send, t_recv, a_send, a_recv, b_send, b_recv,
 ):
-    count = out_ref.shape[0]
+    count = len_ref.shape[0]
     rows = wk_ref.shape[0]
     half_rows = rows // 2
     inverse = 1.0 / math.sqrt(HEAD)
@@ -122,6 +107,34 @@
     beyond = (sib + 2) % 4
     other = g + 1 - 2 * (g % 2)
     half = g % 2
+    b = lax.axis_index("blk")
+    blocks = lax.axis_size("blk")
+    block_rows = test_ref.shape[0]
+    MESH = pl.DeviceIdType.MESH
+
+    def to_block(k):
+        return {"blk": (b + k) % blocks}
+
+    def test_copy(k):
+        where = pl.ds(pl.multiple_of(b * block_rows, block_rows), block_rows)
+        return pltpu.make_async_remote_copy(
+            src_ref=test_ref, dst_ref=tests.at[where, :], send_sem=t_send.at[k],
+            recv_sem=t_recv.at[k], device_id=to_block(k), device_id_type=MESH,
+        )
+
+    def feat_copy(k):
+        part = fbuf.at[f * blocks + b]
+        return pltpu.make_async_remote_copy(
+            src_ref=part, dst_ref=part, send_sem=a_send.at[k],
+            recv_sem=a_recv.at[k], device_id=to_block(k), device_id_type=MESH,
+        )
+
+    def spread_copy(k):
+        part = fbuf.at[pl.ds(f * blocks, blocks)]
+        return pltpu.make_async_remote_copy(
+            src_ref=part, dst_ref=part, send_sem=b_send.at[k],
+            recv_sem=b_recv.at[k], device_id={"fsdp": (f + k) % 4}, device_id_type=MESH,
+        )
 
     def rows_of(owner, part):
         return pl.ds(pl.multiple_of(owner * rows + part * half_rows, half_rows), half_rows)
@@ -160,15 +173,23 @@
         pltpu.make_async_copy(src, dst, in_sem.at[i])
         for i, (src, dst) in enumerate(((hidden_ref, hid), (query_ref, que), (outg_ref, outg)))
     ]
+    own_tests = pltpu.make_async_copy(
+        test_ref, tests.at[pl.ds(pl.multiple_of(b * block_rows, block_rows), block_rows), :], t_sem
+    )
+    own_tests.start()
     for load in loads:
         load.start()
 
     barrier = pltpu.get_barrier_semaphore()
-    for to in (to_sib, to_across, to_other):
-        pl.semaphore_signal(barrier, inc=1, device_id=to, device_id_type=pl.DeviceIdType.MESH)
-    pl.semaphore_wait(barrier, 3)
+    partners = [to_sib, to_across, {"fsdp": beyond}, to_other]
+    partners += [to_block(k) for k in range(1, blocks)]
+    for to in partners:
+        pl.semaphore_signal(barrier, inc=1, device_id=to, device_id_type=MESH)
+    pl.semaphore_wait(barrier, len(partners))
     for h in range(AHEAD):
         send_own(h)
+    for k in range(1, blocks):
+        test_copy(k).start()
 
     loads[0].wait()
     strip = 16
@@ -181,7 +202,9 @@
         return carry
 
     lax.fori_loop(0, hid.shape[0] // strip, normalize, 0)
-    right[...] = jnp.dot(normed[...], pin_ref[...], preferred_element_type=jnp.float32)
+    right[...] = lax.dot_general(
+        normed[...], pin_ref[...], CONTRACT_LAST, preferred_element_type=jnp.float32
+    )
     left[...] = jnp.zeros_like(left)
     loads[1].wait()
     loads[2].wait()
@@ -197,9 +220,8 @@
         keys = both[:, :HEAD]
         keys = (keys * cosine + pltpu.roll(keys, HEAD // 2, 1) * sine).astype(jnp.bfloat16)
         values = both[:, HEAD:].astype(jnp.bfloat16)
-        causal = lax.broadcasted_iota(jnp.int32, (SEQ, GROUP * SEQ), 0) <= (
-            lax.broadcasted_iota(jnp.int32, (SEQ, GROUP * SEQ), 1) % SEQ
-        )
+        places = lax.broadcasted_iota(jnp.int32, (SEQ, GROUP * SEQ), 1) % SEQ
+        causal = lax.broadcasted_iota(jnp.int32, (SEQ, GROUP * SEQ), 0) <= places
         grads = []
         for e in range(count):
             mine = slice(e * SEQ, (e + 1) * SEQ)
@@ -212,14 +234,17 @@
             prob = raised / jnp.sum(raised, axis=0, keepdims=True)
             grad_prob = lax.dot_general(
                 values[mine], stack(outg, e, h), CONTRACT_LAST, preferred_element_type=jnp.float32
-            ) * keep_ref[e : e + 1, :]
+            )
+            grad_prob = jnp.where(places < len_ref[e], grad_prob, 0.0)
             total = jnp.sum(prob * grad_prob, axis=0, keepdims=True)
             grad_logit = (prob * (grad_prob - total)).astype(jnp.bfloat16)
             grads.append(jnp.dot(grad_logit, queries, preferred_element_type=jnp.float32))
         grad = jnp.concatenate(grads, axis=0) * inverse
         grad = grad * cosine + pltpu.roll(grad * sine, HEAD // 2, 1)
-        block = pout_ref[pl.ds(pl.multiple_of(h * HEAD, HEAD), HEAD), :]
-        left[...] += jnp.dot(grad.astype(jnp.bfloat16), block, preferred_element_type=jnp.float32)
+        block = pout_ref[:, pl.ds(pl.multiple_of(h * HEAD, HEAD), HEAD)]
+        left[...] += lax.dot_general(
+            grad.astype(jnp.bfloat16), block, CONTRACT_LAST, preferred_element_type=jnp.float32
+        )
 
     def step(i, carry):
         @pl.when(i < KV_HEADS)
@@ -258,33 +283,64 @@
         return carry
 
     lax.fori_loop(0, KV_HEADS, finish, 0)
-    shape = left.shape
+    shape = (hid.shape[0], PROJ * count)
+    repeats = lax.broadcasted_iota(jnp.int32, (PROJ, PROJ * count), 0) == (
+        lax.broadcasted_iota(jnp.int32, (PROJ, PROJ * count), 1) // count
+    )
+    spread = jnp.dot(
+        left[...], repeats.astype(jnp.float32), precision=HIGHEST, preferred_element_type=jnp.float32
+    )
     belongs = lax.broadcasted_iota(jnp.int32, shape, 0) // SEQ == (
         lax.broadcasted_iota(jnp.int32, shape, 1) % count
     )
     outer = lax.dot_general(
-        jnp.where(belongs, left[...], 0.0),
+        jnp.where(belongs, spread, 0.0),
         right[...],
         (((0,), (0,)), ((), ())),
         precision=HIGHEST,
         preferred_element_type=jnp.float32,
     )
+    slot = f * blocks + b
     for i in range(PROJ):
-        out_ref[:, i * PROJ : (i + 1) * PROJ] = outer[i * count : (i + 1) * count, :]
-
-
-def features_of(hidden, query, out_grad, lengths, gain, w_key, w_value, proj_in, proj_out):
+        fbuf[slot, :, i * PROJ : (i + 1) * PROJ] = outer[i * count : (i + 1) * count, :]
+    for k in range(1, blocks):
+        feat_copy(k).start()
+    for k in range(1, blocks):
+        feat_copy(k).wait_recv()
+    for k in range(1, 4):
+        spread_copy(k).start()
+    own_tests.wait()
+    for k in range(1, blocks):
+        test_copy(k).wait_recv()
+    for k in range(1, 4):
+        spread_copy(k).wait_recv()
+    for i in range(4 * blocks):
+        flat[i * count : (i + 1) * count, :] = fbuf[i]
+    out_ref[...] = score(flat[...], tests[...], inv_ref, slot * count, count)
+    for k in range(1, blocks):
+        test_copy(k).wait_send()
+        feat_copy(k).wait_send()
+    for k in range(1, 4):
+        spread_copy(k).wait_send()
+
+
+def on_device(
+    hidden, query, out_grad, lengths, gain, w_key, w_value, proj_in, proj_out, test_feats
+):
     count = lengths.shape[0]
     tokens, width = hidden.shape
-    keep = (jnp.arange(SEQ)[None, :] < lengths[:, None]).astype(jnp.float32)
+    blocks = lax.axis_size("blk")
+    examples = 4 * blocks * count
     cosine, sine = rope_tables(count)
     anywhere = pl.BlockSpec(memory_space=pl.ANY)
     vmem = pl.BlockSpec(memory_space=pltpu.VMEM)
+    smem = pl.BlockSpec(memory_space=pltpu.SMEM)
     heads = pltpu.SemaphoreType.DMA((KV_HEADS,))
+    queries = blocks * test_feats.shape[0]
     return pl.pallas_call(
-        feature_kernel,
-        out_shape=jax.ShapeDtypeStruct((count, PROJ * PROJ), jnp.float32),
-        in_specs=[anywhere] * 3 + [vmem] * 2 + [anywhere] * 2 + [vmem] * 4,
+        score_kernel,
+        out_shape=jax.ShapeDtypeStruct((count, queries), jnp.float32),
+        in_specs=[anywhere] * 3 + [smem, vmem] + [anywhere] * 2 + [vmem] * 2 + [anywhere] + [vmem] * 2,
         out_specs=vmem,
         scratch_shapes=[
             pltpu.VMEM((KV_HEADS, 2, width, HEAD), jnp.bfloat16),
@@ -292,33 +348,29 @@
             pltpu.VMEM((tokens, query.shape[1]), jnp.bfloat16),
             pltpu.VMEM((tokens, query.shape[1]), jnp.bfloat16),
             pltpu.VMEM((tokens, width), jnp.bfloat16),
-            pltpu.VMEM((tokens, PROJ * count), jnp.float32),
             pltpu.VMEM((tokens, PROJ), jnp.float32),
+            pltpu.VMEM((tokens, PROJ), jnp.float32),
+            pltpu.VMEM((4 * blocks, count, PROJ * PROJ), jnp.float32),
+            pltpu.VMEM((examples, PROJ * PROJ), jnp.float32),
+            pltpu.VMEM((queries, PROJ * PROJ), jnp.bfloat16),
+            pltpu.VMEM((examples, examples), jnp.float32),
             pltpu.SemaphoreType.DMA((3,)),
             pltpu.SemaphoreType.DMA((2, KV_HEADS)),
         ]
-        + [heads] * 10,
+        + [heads] * 10
+        + [pltpu.SemaphoreType.DMA]
+        + [pltpu.SemaphoreType.DMA((blocks,))] * 4
+        + [pltpu.SemaphoreType.DMA((4,))] * 2,
         compiler_params=pltpu.CompilerParams(
-            collective_id=0, has_side_effects=True, vmem_limit_bytes=56 * 1024 * 1024
+            collective_id=0, has_side_effects=True, vmem_limit_bytes=58 * 1024 * 1024
         ),
         cost_estimate=pl.CostEstimate(
             flops=2 * tokens * width * 2 * KV_HEADS * HEAD, bytes_accessed=100_000_000, transcendentals=0
         ),
     )(
-        hidden, query, out_grad, jnp.tile(keep, (1, GROUP)), gain.reshape(1, width), w_key, w_value,
-        proj_in, jnp.repeat(proj_out, count, axis=1), cosine, sine,
-    )
-
-
-def on_device(
-    hidden, query, out_grad, lengths, gain, w_key, w_value, proj_in, proj_out, test_feats
-):
-    features = features_of(
-        hidden, query, out_grad, lengths, gain, w_key, w_value, proj_in, proj_out
-    )
-    every_feat = lax.all_gather(features, ("blk", "fsdp"), axis=0, tiled=True)
-    tests = lax.all_gather(test_feats, "blk", axis=0, tiled=True)
-    return score(every_feat, tests, features.shape[0])
+        hidden, query, out_grad, lengths, gain.reshape(1, width), w_key, w_value,
+        proj_in.T, proj_out.T, test_feats, cosine, sine,
+    )
 
 
 def solution(mesh):

time: 115 us -> 83.7 us (0.73)
  blocking collectives: 22.4 us -> 0 us
  between operations: 13.4 us -> 0.01 us
  Pallas kernels: 72.2 us -> 82.2 us
  local copies, waits for them, and re-layouts: 6.12 us -> 1.3 us
    all_gather x1 -> x0, blocking collectives: 22.4 us -> none  [on_device(): every_feat = lax.all_gather(features, ('blk', 'fsdp'), axis=0, tiled=True)]
    pallas_call x2 -> x1, Pallas kernels: 72.2 us -> 82.2 us  [on_device(): pl.pallas_call(score_kernel, out_shape=jax.ShapeDtypeStruct((count, queri...]
    unnamed x6 -> x1, local copies, waits for them, and re-layouts: 3.62 us -> 1.3 us
  transfers between devices with their start and end apart: 1 -> 0, of which waited for: 0 -> 0; matrix products, arithmetic and copies ran while one was open for 4% -> 0% of each run, Pallas kernels for 55% -> 0%
where the time goes in v2:
time: 83.7 us; the launch traced here: 83.5 us
  Pallas kernels  82.2 us (98%)
  local copies, waits for them, and re-layouts  1.3 us (2%)
    pallas_call x1, Pallas kernels, on_device(): pl.pallas_call(score_kernel, out_shape=jax.ShapeDtypeStruct((count, queri...  82.2 us

profile of v2, /device:TPU:1, one launch (start us, length us, event | category | flops | bytes accessed | tf_op | source)
XLA Modules:
  0.0 83.5 jit_solution(3426125006772495343)
XLA Ops:
  0.0 82.2 %shard_map.118 = f32[4,512]{1,0:T(4,128)} custom-call(bf16[256,4096]{1,0:T(8,128)(2,1)} %hidden_ref.1, bf16[256,4096]{1,0:T(8,128)(2,1)} %query_ref.1, bf16[256,4096]{1,0:T(8,128)(2,1)} %outg_ref.1, s32[4]{0:T(128)} %len_ref.1, f32[1,4096]{1,0:T(1,128)} %bitcast.5, bf16[1024,1024]{1,0:T(8,128)(2,1)} %wk_ref.1, bf16[1024,1024]{1,0:T(8,128)(2,1)} %wv_ref.1, ...), custom_call_target="tpu_custom_call" | custom-call | flops 4294967296 | bytes 100000000 | tf_op jit(solution)/shard_map/pallas_call | solution.py:340
  82.2 1.3 %copy.14 = f32[4,512]{1,0:T(4,128)} copy(f32[4,512]{1,0:T(4,128)} %shard_map.118) | data formatting | bytes 16384

commit v3 on v2

--- a/solution.py
+++ b/solution.py
@@ -19,7 +19,8 @@
 rope_base = 500000.0
 damping = 0.01
 GROUP = HEADS // KV_HEADS
-AHEAD = 2
+AHEAD = 3
+SIB, X, X_FAR, Y, Z, Y_FAR, S_X, S_X_FAR, S_Y, S_Z, S_Y_FAR = range(11)
 
 
 def rope_tables(count):
@@ -92,13 +93,11 @@
     hidden_ref, query_ref, outg_ref, len_ref, gain_ref, wk_ref, wv_ref, pin_ref, pout_ref,
     test_ref, cos_ref, sin_ref, out_ref,
     wbuf, hid, que, outg, normed, left, right, fbuf, flat, tests, inv_ref,
-    in_sem, own_sem, sib_send, sib_recv, x_send, x_recv, y_send, y_recv,
-    fx_send, fx_recv, fy_send, fy_recv,
-    t_sem, t_send, t_recv, a_send, a_recv, b_send, b_recv,
+    in_sem, own_sem, sends, recvs, t_sem, t_send, t_recv, u_send, u_recv, a_send, a_recv, b_send, b_recv,
 ):
     count = len_ref.shape[0]
     rows = wk_ref.shape[0]
-    half_rows = rows // 2
+    eighth = rows // 8
     inverse = 1.0 / math.sqrt(HEAD)
     g = lax.axis_index("groups")
     f = lax.axis_index("fsdp")
@@ -106,7 +105,6 @@
     across = (f + 2) % 4
     beyond = (sib + 2) % 4
     other = g + 1 - 2 * (g % 2)
-    half = g % 2
     b = lax.axis_index("blk")
     blocks = lax.axis_size("blk")
     block_rows = test_ref.shape[0]
@@ -115,11 +113,25 @@
     def to_block(k):
         return {"blk": (b + k) % blocks}
 
+    beside = b + 1 - 2 * (b % 2)
+    half_block = block_rows // 2
+
+    def test_rows(block):
+        start = block * block_rows + (f % 2) * half_block
+        return tests.at[pl.ds(pl.multiple_of(start, half_block), half_block), :]
+
     def test_copy(k):
-        where = pl.ds(pl.multiple_of(b * block_rows, block_rows), block_rows)
+        start = pl.multiple_of((f % 2) * half_block, half_block)
         return pltpu.make_async_remote_copy(
-            src_ref=test_ref, dst_ref=tests.at[where, :], send_sem=t_send.at[k],
-            recv_sem=t_recv.at[k], device_id=to_block(k), device_id_type=MESH,
+            src_ref=test_ref.at[pl.ds(start, half_block), :], dst_ref=test_rows(b),
+            send_sem=t_send.at[k], recv_sem=t_recv.at[k], device_id=to_block(k), device_id_type=MESH,
+        )
+
+    def test_pass(k):
+        part = test_rows((b + blocks - k) % blocks)
+        return pltpu.make_async_remote_copy(
+            src_ref=part, dst_ref=part, send_sem=u_send.at[k], recv_sem=u_recv.at[k],
+            device_id=to_sib, device_id_type=MESH,
         )
 
     def feat_copy(k):
@@ -136,19 +148,61 @@
             recv_sem=b_recv.at[k], device_id={"fsdp": (f + k) % 4}, device_id_type=MESH,
         )
 
-    def rows_of(owner, part):
-        return pl.ds(pl.multiple_of(owner * rows + part * half_rows, half_rows), half_rows)
-
-    def copy(h, where, send, recv, to):
+    mine = 2 * (g % 2) + b % 2
+    by_y = 2 * (1 - g % 2) + b % 2
+    by_z = 2 * (g % 2) + 1 - b % 2
+    far = 2 * (1 - g % 2) + 1 - b % 2
+
+    def rows_of(owner, quarter, part=None):
+        start = owner * rows + quarter * 2 * eighth + (part or 0) * eighth
+        return pl.ds(pl.multiple_of(start, eighth), eighth * (2 if part is None else 1))
+
+    def copy(h, where, kind, to):
         part = wbuf.at[h, :, where, :]
         return pltpu.make_async_remote_copy(
-            src_ref=part, dst_ref=part, send_sem=send.at[h], recv_sem=recv.at[h],
-            device_id=to, device_id_type=pl.DeviceIdType.MESH,
+            src_ref=part, dst_ref=part, send_sem=sends.at[kind, h], recv_sem=recvs.at[kind, h],
+            device_id=to, device_id_type=MESH,
         )
 
     whole_own = pl.ds(pl.multiple_of(f * rows, rows), rows)
     whole_sib = pl.ds(pl.multiple_of(sib * rows, rows), rows)
-    to_sib, to_across, to_other = {"fsdp": sib}, {"fsdp": across}, {"groups": other}
+    to_sib, to_across = {"fsdp": sib}, {"fsdp": across}
+    to_other, to_beside = {"groups": other}, {"blk": beside}
+    sent = {
+        SIB: (whole_own, to_sib),
+        X: (rows_of(f, mine), to_across),
+        X_FAR: (rows_of(f, far, 0), to_across),
+        Y: (rows_of(across, mine), to_other),
+        Z: (rows_of(across, mine), to_beside),
+        Y_FAR: (rows_of(across, by_z, 1), to_other),
+        S_X: (rows_of(across, mine), to_sib),
+        S_X_FAR: (rows_of(across, far, 0), to_sib),
+        S_Y: (rows_of(across, by_y), to_sib),
+        S_Z: (rows_of(across, by_z), to_sib),
+        S_Y_FAR: (rows_of(across, far, 1), to_sib),
+    }
+    received = {
+        SIB: whole_sib,
+        X: rows_of(across, mine),
+        X_FAR: rows_of(across, far, 0),
+        Y: rows_of(across, by_y),
+        Z: rows_of(across, by_z),
+        Y_FAR: rows_of(across, far, 1),
+        S_X: rows_of(beyond, mine),
+        S_X_FAR: rows_of(beyond, far, 0),
+        S_Y: rows_of(beyond, by_y),
+        S_Z: rows_of(beyond, by_z),
+        S_Y_FAR: rows_of(beyond, far, 1),
+    }
+
+    def start(h, *kinds):
+        for kind in kinds:
+            where, to = sent[kind]
+            copy(h, where, kind, to).start()
+
+    def arrive(h, *kinds):
+        for kind in kinds:
+            copy(h, received[kind], kind, sent[kind][1]).wait_recv()
 
     def own(h, kind):
         return pltpu.make_async_copy(
@@ -160,14 +214,18 @@
     def send_own(h):
         own(h, 0).wait()
         own(h, 1).wait()
-        copy(h, rows_of(f, half), x_send, x_recv, to_across).start()
-        copy(h, whole_own, sib_send, sib_recv, to_sib).start()
+        start(h, X, X_FAR, SIB)
 
     def start_own(h, carry):
         own(h, 0).start()
         own(h, 1).start()
         return carry
 
+    barrier = pltpu.get_barrier_semaphore()
+    partners = [to_sib, to_across, {"fsdp": beyond}, to_other]
+    partners += [to_block(k) for k in range(1, blocks)]
+    for to in partners:
+        pl.semaphore_signal(barrier, inc=1, device_id=to, device_id_type=MESH)
     lax.fori_loop(0, KV_HEADS, start_own, 0)
     loads = [
         pltpu.make_async_copy(src, dst, in_sem.at[i])
@@ -180,16 +238,9 @@
     for load in loads:
         load.start()
 
-    barrier = pltpu.get_barrier_semaphore()
-    partners = [to_sib, to_across, {"fsdp": beyond}, to_other]
-    partners += [to_block(k) for k in range(1, blocks)]
-    for to in partners:
-        pl.semaphore_signal(barrier, inc=1, device_id=to, device_id_type=MESH)
     pl.semaphore_wait(barrier, len(partners))
     for h in range(AHEAD):
         send_own(h)
-    for k in range(1, blocks):
-        test_copy(k).start()
 
     loads[0].wait()
     strip = 16
@@ -249,25 +300,39 @@
     def step(i, carry):
         @pl.when(i < KV_HEADS)
         def _():
-            copy(i, rows_of(across, half), x_send, x_recv, to_across).wait_recv()
-            copy(i, rows_of(across, half), y_send, y_recv, to_other).start()
-            copy(i, rows_of(across, half), fx_send, fx_recv, to_sib).start()
+            arrive(i, X)
+            start(i, Y, Z, S_X)
+            arrive(i, X_FAR)
+            start(i, S_X_FAR)
 
         @pl.when(i + AHEAD < KV_HEADS)
         def _():
             send_own(i + AHEAD)
 
+        @pl.when(i == KV_HEADS // 2)
+        def _():
+            for k in range(1, blocks):
+                test_copy(k).start()
+
         @pl.when((i >= 1) & (i <= KV_HEADS))
         def _():
-            copy(i - 1, rows_of(across, 1 - half), y_send, y_recv, to_other).wait_recv()
-            copy(i - 1, rows_of(across, 1 - half), fy_send, fy_recv, to_sib).start()
+            arrive(i - 1, Z)
+            start(i - 1, Y_FAR, S_Z)
+            arrive(i - 1, Y)
+            start(i - 1, S_Y)
+
+        @pl.when(i > KV_HEADS)
+        def _():
+            for k in range(1, blocks):
+                test_copy(k).wait_recv()
+                test_pass(k).start()
 
         @pl.when(i >= 2)
         def _():
             h = i - 2
-            copy(h, whole_sib, sib_send, sib_recv, to_sib).wait_recv()
-            copy(h, rows_of(beyond, half), fx_send, fx_recv, to_sib).wait_recv()
-            copy(h, rows_of(beyond, 1 - half), fy_send, fy_recv, to_sib).wait_recv()
+            arrive(h, Y_FAR)
+            start(h, S_Y_FAR)
+            arrive(h, SIB, S_X, S_X_FAR, S_Y, S_Z, S_Y_FAR)
             head(h)
 
         return carry
@@ -275,11 +340,8 @@
     lax.fori_loop(0, KV_HEADS + 2, step, 0)
 
     def finish(h, carry):
-        copy(h, rows_of(f, half), x_send, x_recv, to_across).wait_send()
-        copy(h, whole_own, sib_send, sib_recv, to_sib).wait_send()
-        copy(h, rows_of(across, half), y_send, y_recv, to_other).wait_send()
-        copy(h, rows_of(across, half), fx_send, fx_recv, to_sib).wait_send()
-        copy(h, rows_of(across, 1 - half), fy_send, fy_recv, to_sib).wait_send()
+        for kind, (where, to) in sent.items():
+            copy(h, where, kind, to).wait_send()
         return carry
 
     lax.fori_loop(0, KV_HEADS, finish, 0)
@@ -311,7 +373,7 @@
         spread_copy(k).start()
     own_tests.wait()
     for k in range(1, blocks):
-        test_copy(k).wait_recv()
+        test_pass(k).wait_recv()
     for k in range(1, 4):
         spread_copy(k).wait_recv()
     for i in range(4 * blocks):
@@ -319,6 +381,7 @@
     out_ref[...] = score(flat[...], tests[...], inv_ref, slot * count, count)
     for k in range(1, blocks):
         test_copy(k).wait_send()
+        test_pass(k).wait_send()
         feat_copy(k).wait_send()
     for k in range(1, 4):
         spread_copy(k).wait_send()
@@ -335,7 +398,6 @@
     anywhere = pl.BlockSpec(memory_space=pl.ANY)
     vmem = pl.BlockSpec(memory_space=pltpu.VMEM)
     smem = pl.BlockSpec(memory_space=pltpu.SMEM)
-    heads = pltpu.SemaphoreType.DMA((KV_HEADS,))
     queries = blocks * test_feats.shape[0]
     return pl.pallas_call(
         score_kernel,
@@ -357,9 +419,9 @@
             pltpu.SemaphoreType.DMA((3,)),
             pltpu.SemaphoreType.DMA((2, KV_HEADS)),
         ]
-        + [heads] * 10
+        + [pltpu.SemaphoreType.DMA((11, KV_HEADS))] * 2
         + [pltpu.SemaphoreType.DMA]
-        + [pltpu.SemaphoreType.DMA((blocks,))] * 4
+        + [pltpu.SemaphoreType.DMA((blocks,))] * 6
         + [pltpu.SemaphoreType.DMA((4,))] * 2,
         compiler_params=pltpu.CompilerParams(
             collective_id=0, has_side_effects=True, vmem_limit_bytes=58 * 1024 * 1024

time: 83.7 us -> 82.8 us (0.989)
  Pallas kernels: 82.2 us -> 81.3 us
    pallas_call x1, Pallas kernels: 82.2 us -> 81.3 us  [on_device(): pl.pallas_call(score_kernel, out_shape=jax.ShapeDtypeStruct((count, queri...]
where the time goes in v3:
time: 82.8 us; the launch traced here: 82.6 us
  Pallas kernels  81.3 us (98%)
  local copies, waits for them, and re-layouts  1.3 us (2%)
    pallas_call x1, Pallas kernels, on_device(): pl.pallas_call(score_kernel, out_shape=jax.ShapeDtypeStruct((count, queri...  81.3 us

profile of v3, /device:TPU:1, one launch (start us, length us, event | category | flops | bytes accessed | tf_op | source)
XLA Modules:
  0.0 82.6 jit_solution(2559723355056092156)
XLA Ops:
  0.0 81.3 %shard_map.118 = f32[4,512]{1,0:T(4,128)} custom-call(bf16[256,4096]{1,0:T(8,128)(2,1)} %hidden_ref.1, bf16[256,4096]{1,0:T(8,128)(2,1)} %query_ref.1, bf16[256,4096]{1,0:T(8,128)(2,1)} %outg_ref.1, s32[4]{0:T(128)} %len_ref.1, f32[1,4096]{1,0:T(1,128)} %bitcast.5, bf16[1024,1024]{1,0:T(8,128)(2,1)} %wk_ref.1, bf16[1024,1024]{1,0:T(8,128)(2,1)} %wv_ref.1, ...), custom_call_target="tpu_custom_call" | custom-call | flops 4294967296 | bytes 100000000 | tf_op jit(solution)/shard_map/pallas_call | solution.py:402
  81.3 1.3 %copy.14 = f32[4,512]{1,0:T(4,128)} copy(f32[4,512]{1,0:T(4,128)} %shard_map.118) | data formatting | bytes 16384

commit v4 on v3

--- a/solution.py
+++ b/solution.py
@@ -314,30 +314,34 @@
             for k in range(1, blocks):
                 test_copy(k).start()
 
-        @pl.when((i >= 1) & (i <= KV_HEADS))
-        def _():
-            arrive(i - 1, Z)
-            start(i - 1, Y_FAR, S_Z)
-            arrive(i - 1, Y)
-            start(i - 1, S_Y)
-
-        @pl.when(i > KV_HEADS)
+        @pl.when((i >= 2) & (i < KV_HEADS + 2))
+        def _():
+            arrive(i - 2, Z)
+            start(i - 2, Y_FAR, S_Z)
+            arrive(i - 2, Y)
+            start(i - 2, S_Y)
+
+        @pl.when(i == KV_HEADS + 1)
         def _():
             for k in range(1, blocks):
                 test_copy(k).wait_recv()
                 test_pass(k).start()
 
-        @pl.when(i >= 2)
-        def _():
-            h = i - 2
+        @pl.when((i >= 3) & (i < KV_HEADS + 3))
+        def _():
+            h = i - 3
             arrive(h, Y_FAR)
             start(h, S_Y_FAR)
+
+        @pl.when(i >= 4)
+        def _():
+            h = i - 4
             arrive(h, SIB, S_X, S_X_FAR, S_Y, S_Z, S_Y_FAR)
             head(h)
 
         return carry
 
-    lax.fori_loop(0, KV_HEADS + 2, step, 0)
+    lax.fori_loop(0, KV_HEADS + 4, step, 0)
 
     def finish(h, carry):
         for kind, (where, to) in sent.items():

time: 82.8 us -> 77.8 us (0.940)
  Pallas kernels: 81.3 us -> 76.2 us
    pallas_call x1, Pallas kernels: 81.3 us -> 76.2 us  [on_device(): pl.pallas_call(score_kernel, out_shape=jax.ShapeDtypeStruct((count, queri...]
where the time goes in v4:
time: 77.8 us; the launch traced here: 77.5 us
  Pallas kernels  76.2 us (98%)
  local copies, waits for them, and re-layouts  1.3 us (2%)
    pallas_call x1, Pallas kernels, on_device(): pl.pallas_call(score_kernel, out_shape=jax.ShapeDtypeStruct((count, queri...  76.2 us

profile of v4, /device:TPU:1, one launch (start us, length us, event | category | flops | bytes accessed | tf_op | source)
XLA Modules:
  0.0 77.5 jit_solution(18184205756460021894)
XLA Ops:
  0.0 76.2 %shard_map.118 = f32[4,512]{1,0:T(4,128)} custom-call(bf16[256,4096]{1,0:T(8,128)(2,1)} %hidden_ref.1, bf16[256,4096]{1,0:T(8,128)(2,1)} %query_ref.1, bf16[256,4096]{1,0:T(8,128)(2,1)} %outg_ref.1, s32[4]{0:T(128)} %len_ref.1, f32[1,4096]{1,0:T(1,128)} %bitcast.5, bf16[1024,1024]{1,0:T(8,128)(2,1)} %wk_ref.1, bf16[1024,1024]{1,0:T(8,128)(2,1)} %wv_ref.1, ...), custom_call_target="tpu_custom_call" | custom-call | flops 4294967296 | bytes 100000000 | tf_op jit(solution)/shard_map/pallas_call | solution.py:406
  76.3 1.3 %copy.14 = f32[4,512]{1,0:T(4,128)} copy(f32[4,512]{1,0:T(4,128)} %shard_map.118) | data formatting | bytes 16384
